TPU v7x, 512 devices: a whole 4x8x8 slice. The times are simulated.
512 devices in a mesh: pair: 16 (over z_lo, y), row: 4 (over x), col: 8 (over z_hi, core).
Axes of the slice: x: 4, y: 8, z: 8 (z_hi: 4, z_lo: 2; z = z_hi * 2 + z_lo), core: 2. Of those that a mesh axis runs over, the one named last changes fastest.
Arguments:
- integrals: bfloat16 [12288, 4096], P(('pair', 'col')), may hold values from -0.21875 to 0.21875
- inverse_factor: bfloat16 [4096, 4096], P('row', ('pair', 'col')), may hold values from -4 to 4, as said below
- energies: float32 [12288], P('pair'), may hold values from 0.25 to 8
- frequency: float32 [1], replicated, may hold values from 0.5 to 2
Outputs:
- response: float32 [4096, 4096], P(('row', 'pair'), 'col')
Inputs may be any that keep to these rules, and one draw needn't show every extreme that they name: `inverse_factor`: zero above the diagonal; the diagonal lies between 0.5 and 3.
All inputs are finite; a program needn't handle non-finite values.
Results may differ from a plain program's by a relative error of at most 0.0025.
Values may be sent and summed in bfloat16 or wider, within the bound.
A program may use at most 64 MiB of HBM per device.

v0:
```python
import jax
import jax.numpy as jnp
from jax import lax
from jax.sharding import PartitionSpec as P


def contract(x_columns, portion):
    return lax.dot_general(
        x_columns, portion, (((1,), (1,)), ((), ())), preferred_element_type=jnp.float32
    )


def on_device(integrals, inverse_factor, energies, frequency):
    n_col = lax.axis_size("col")
    aux_width = integrals.shape[1]
    q_cols = aux_width // n_col
    local_rows = contract(
        integrals, lax.all_gather(inverse_factor, ("pair", "col"), axis=1, tiled=True)
    )
    group_b = lax.all_gather(local_rows.astype(jnp.bfloat16), "col", axis=0, tiled=True)
    col_position = lax.axis_index("col")
    empty = jnp.zeros((group_b.shape[0], q_cols), jnp.bfloat16)
    portion = lax.all_gather(group_b, "row", axis=1, tiled=True)
    portion_width = portion.shape[1]
    wanted = col_position * q_cols + jnp.arange(q_cols, dtype=jnp.int32)
    inside = (wanted >= 0) & (wanted < portion_width)
    selected = jnp.take(portion, jnp.clip(wanted, 0, portion_width - 1), axis=1)
    col_b = jnp.where(inside[None, :], selected, empty)
    factor = 2.0 * energies / (energies * energies + frequency[0] * frequency[0])
    scaled = (factor[:, None] * group_b.astype(jnp.float32)).astype(jnp.bfloat16)
    return lax.psum_scatter(
        lax.dot_general(
            scaled, col_b, (((0,), (0,)), ((), ())), preferred_element_type=jnp.float32
        ),
        "pair",
        scatter_dimension=0,
        tiled=True,
    )


def solution(mesh):
    return jax.shard_map(
        on_device,
        mesh=mesh,
        in_specs=(P(("pair", "col"), None), P("row", ("pair", "col")), P("pair"), P()),
        out_specs=P(("row", "pair"), "col"),
        check_vma=False,
    )
```

profile of v0, /device:TPU:2, one launch (start us, length us, event | category | flops | bytes accessed | tf_op | source)
XLA Modules:
  0.0 452.1 jit_solution(15941670298254573152)
XLA Ops:
  6.5 0.0 copy-start
  6.5 0.0 all-gather.4.cloned.1.call-start
  6.5 0.7 all-gather.4.cloned.1.call-update
  7.3 0.0 copy-start.2
  7.3 0.0 all-gather.6.cloned.1.call-start
  7.3 231.2 %all-gather.4.cloned.1.call-done = bf16[1024,4096]{0,1:T(8,128)(2,1)} async-done(((bf16[1024,32]{0,1:T(8,128)(2,1)}), bf16[1024,4096]{0,1:T(8,128)(2,1)}) %all-gather.4.cloned.1.call-update) | async-done | bytes 8388624 | tf_op jit(solution)/shard_map/all_gather | solution.py:18
  238.5 0.0 copy-done
  238.5 5.5 %convolution_convert_fusion = bf16[96,1024]{1,0:T(8,128)(2,1)} fusion(bf16[96,4096]{1,0:T(8,128)(2,1)S(1)} %copy-done, bf16[1024,4096]{0,1:T(8,128)(2,1)} %all-gather.4.cloned.1.call-done), kind=kOutput, calls=%fused_computation.4 | convolution fusion | flops 805404672 | bytes 9371648 | tf_op jit(solution)/shard_map/dot_general | solution.py:8
  244.0 0.0 all-gather.6.cloned.1.call-update
  244.0 0.0 all-gather.8.cloned.1.call-start
  244.1 35.0 %all-gather.6.cloned.1.call-done = bf16[768,1024]{1,0:T(8,128)(2,1)} async-done(((bf16[96,1024]{1,0:T(8,128)(2,1)}), bf16[768,1024]{1,0:T(8,128)(2,1)}) %all-gather.6.cloned.1.call-update) | async-done | bytes 1572880 | tf_op jit(solution)/shard_map/all_gather | solution.py:20
  279.1 0.0 all-gather.8.cloned.1.call-update
  279.1 0.0 reduce-scatter.2.cloned.1.call-start
  279.8 0.0 copy-done.2
  279.9 70.2 %all-gather.8.cloned.1.call-done = bf16[768,4096]{1,0:T(8,128)(2,1)} async-done(((bf16[768,1024]{1,0:T(8,128)(2,1)}), bf16[768,4096]{1,0:T(8,128)(2,1)}) %all-gather.8.cloned.1.call-update) | async-done | bytes 6291472 | tf_op jit(solution)/shard_map/all_gather | solution.py:23
  350.1 8.7 %copy.6 = bf16[768,4096]{0,1:T(8,128)(2,1)} copy(bf16[768,4096]{1,0:T(8,128)(2,1)} %all-gather.8.cloned.1.call-done) | data formatting | bytes 12582912 | tf_op jit(solution)/shard_map/all_gather | solution.py:23
  358.8 0.0 copy-start.1
  358.8 6.1 %gather_fusion = bf16[512,768]{1,0:T(8,128)(2,1)S(1)} fusion(bf16[768,4096]{0,1:T(8,128)(2,1)} %copy.6, s32[1024]{0:T(1024)S(1)} %pad_clamp_fusion), kind=kCustom, calls=%fused_computation | custom fusion | bytes 1574912 | tf_op jit(solution)/shard_map/jit(_take)/gather | solution.py:27
  364.9 0.0 copy-done.1
  364.9 2.7 fusion
  367.5 0.0 reduce-scatter.2.cloned.1.call-update
  367.6 78.0 %reduce-scatter.2.cloned.1.call-done = f32[64,512]{1,0:T(8,128)} async-done(((f32[1024,512]{1,0:T(8,128)}), f32[64,512]{1,0:T(8,128)}) %reduce-scatter.2.cloned.1.call-update) | async-done | bytes 131088 | tf_op jit(solution)/shard_map/reduce_scatter | solution.py:31
  (4 shorter events, 0.0 us)
Async XLA Ops:
  6.5 231.9 %copy-start = (bf16[96,4096]{1,0:T(8,128)(2,1)S(1)}, bf16[96,4096]{1,0:T(8,128)(2,1)}, u32[]{:S(2)}) copy-start(bf16[96,4096]{1,0:T(8,128)(2,1)} %param.4) | copy-start | bytes 2359300
  6.5 231.9 %all-gather.4.cloned.1.call-start = ((), (), s32[]{:S(2)}) async-start(), calls=%async_computation.1 | async-start | bytes 8454144 | tf_op jit(solution)/shard_map/all_gather | solution.py:18
  7.3 272.6 %copy-start.2 = (f32[768]{0:T(1024)S(1)}, f32[768]{0:T(1024)}, u32[]{:S(2)}) copy-start(f32[768]{0:T(1024)} %param.6) | copy-start | bytes 9220
  7.3 271.8 %all-gather.6.cloned.1.call-start = ((), (), s32[]{:S(2)}) async-start(), calls=%async_computation.2 | async-start | bytes 1769472 | tf_op jit(solution)/shard_map/all_gather | solution.py:20
  244.0 106.1 %all-gather.8.cloned.1.call-start = ((), (), s32[]{:S(2)}) async-start(), calls=%async_computation.3 | async-start | bytes 7864320 | tf_op jit(solution)/shard_map/all_gather | solution.py:23
  279.1 166.5 %reduce-scatter.2.cloned.1.call-start = ((), (), s32[]{:S(2)}) async-start(), calls=%async_computation.4 | async-start | bytes 2228224 | tf_op jit(solution)/shard_map/reduce_scatter | solution.py:31
  358.8 6.1 %copy-start.1 = (bf16[768,1024]{1,0:T(8,128)(2,1)S(1)}, bf16[768,1024]{1,0:T(8,128)(2,1)}, u32[]{:S(2)}) copy-start(bf16[768,1024]{1,0:T(8,128)(2,1)} %all-gather.6.cloned.1.call-done) | copy-start | bytes 4718596
Sparse Core Ops, SparseCore 0:
  9.5 228.9 all-gather.3
  244.2 34.8 all-gather.5
  281.2 68.8 all-gather.7
  367.7 77.8 reduce-scatter.1
where the time goes:
time: 452 us
  waiting for transfers between devices  415 us (92%)
  local copies, waits for them, and re-layouts  14.8 us (3%)
  between operations  13.8 us (3%)
  matrix products  8.18 us (2%)
    all_gather x1, waiting for transfers between devices, on_device(): lax.all_gather(inverse_factor, ('pair', 'col'), axis=1, tiled=True)  231 us
    reduce_scatter x1, waiting for transfers between devices, on_device(): lax.psum_scatter(lax.dot_general(scaled, col_b, (((0,), (0,)), ((), ())),...  78 us
    all_gather x1, waiting for transfers between devices, on_device(): portion = lax.all_gather(group_b, 'row', axis=1, tiled=True)  70.2 us
    all_gather x1, waiting for transfers between devices, on_device(): lax.all_gather(local_rows.astype(jnp.bfloat16), 'col', axis=0, tiled=True)  35 us
  transfers between devices with their start and end apart: 4, of which 4 were waited for; matrix products, arithmetic and copies ran while one was open for 0% of the time, Pallas kernels for 0%

commit v1 on v0

--- a/solution.py
+++ b/solution.py
@@ -20,7 +20,12 @@
     group_b = lax.all_gather(local_rows.astype(jnp.bfloat16), "col", axis=0, tiled=True)
     col_position = lax.axis_index("col")
     empty = jnp.zeros((group_b.shape[0], q_cols), jnp.bfloat16)
-    portion = lax.all_gather(group_b, "row", axis=1, tiled=True)
+    ring = [group_b]
+    for hop in range(3):
+        ring.append(lax.ppermute(ring[-1], "row", [(dev, (dev + 1) % 4) for dev in range(4)]))
+    portion = jnp.roll(
+        jnp.concatenate(ring[::-1], axis=1), (lax.axis_index("row") + 1) * ring[0].shape[1], axis=1
+    )
     portion_width = portion.shape[1]
     wanted = col_position * q_cols + jnp.arange(q_cols, dtype=jnp.int32)
     inside = (wanted >= 0) & (wanted < portion_width)

time: 452 us -> 506 us (1.12)
  waiting for transfers between devices: 415 us -> 446 us
  local copies, waits for them, and re-layouts: 14.8 us -> 27 us
  starting transfers between devices: 0.12 us -> 10.2 us
    ppermute x0 -> x3, waiting for transfers between devices: none -> 104 us  [on_device(): lax.ppermute(ring[-1], 'row', [(dev, (dev + 1) % 4) for dev in range(4)])]
    all_gather x1 -> x0, waiting for transfers between devices: 70.2 us -> none  [on_device(): portion = lax.all_gather(group_b, 'row', axis=1, tiled=True)]
    dynamic_slice x0 -> x2, local copies, waits for them, and re-layouts: none -> 11.7 us  [on_device(): jnp.roll(jnp.concatenate(ring[::-1], axis=1), (lax.axis_index('row') + 1)...]
    ppermute x0 -> x3, starting transfers between devices: none -> 10.1 us  [on_device(): lax.ppermute(ring[-1], 'row', [(dev, (dev + 1) % 4) for dev in range(4)])]
    unnamed x6 -> x17, local copies, waits for them, and re-layouts: 0.01 us -> 9.21 us
    all_gather x1 -> x0, local copies, waits for them, and re-layouts: 8.65 us -> none  [on_device(): portion = lax.all_gather(group_b, 'row', axis=1, tiled=True)]
  transfers between devices with their start and end apart: 4 -> 6, of which waited for: 4 -> 6; matrix products, arithmetic and copies ran while one was open for 0% -> 0% of each run, Pallas kernels for 0% -> 0%
where the time goes in v1:
time: 506 us; the launch traced here: 505 us
  waiting for transfers between devices  446 us (88%)
  local copies, waits for them, and re-layouts  27 us (5%)
  between operations  13.9 us (3%)
  starting transfers between devices  10.2 us (2%)
  matrix products  8.18 us (2%)
    all_gather x1, waiting for transfers between devices, on_device(): lax.all_gather(inverse_factor, ('pair', 'col'), axis=1, tiled=True)  231 us
    ppermute x3, waiting for transfers between devices, on_device(): lax.ppermute(ring[-1], 'row', [(dev, (dev + 1) % 4) for dev in range(4)])  104 us
    reduce_scatter x1, waiting for transfers between devices, on_device(): lax.psum_scatter(lax.dot_general(scaled, col_b, (((0,), (0,)), ((), ())),...  74.5 us
    all_gather x1, waiting for transfers between devices, on_device(): lax.all_gather(local_rows.astype(jnp.bfloat16), 'col', axis=0, tiled=True)  35 us
    dynamic_slice x2, local copies, waits for them, and re-layouts, on_device(): jnp.roll(jnp.concatenate(ring[::-1], axis=1), (lax.axis_index('row') + 1)...  11.7 us
    ppermute x3, starting transfers between devices, on_device(): lax.ppermute(ring[-1], 'row', [(dev, (dev + 1) % 4) for dev in range(4)])  10.1 us
  transfers between devices with their start and end apart: 6, of which 6 were waited for; matrix products, arithmetic and copies ran while one was open for 0% of the time, Pallas kernels for 0%

profile of v1, /device:TPU:2, one launch (start us, length us, event | category | flops | bytes accessed | tf_op | source)
XLA Modules:
  0.0 505.1 jit_solution(11416987064743607198)
XLA Ops:
  6.5 0.7 all-gather.3.cloned.1.call-update
  7.3 231.2 %all-gather.3.cloned.1.call-done = bf16[1024,4096]{0,1:T(8,128)(2,1)} async-done(((bf16[1024,32]{0,1:T(8,128)(2,1)}), bf16[1024,4096]{0,1:T(8,128)(2,1)}) %all-gather.3.cloned.1.call-update) | async-done | bytes 8388624 | tf_op jit(solution)/shard_map/all_gather | solution.py:18
  238.5 5.5 %convolution_convert_fusion = bf16[96,1024]{1,0:T(8,128)(2,1)} fusion(bf16[96,4096]{1,0:T(8,128)(2,1)S(1)} %copy-done, bf16[1024,4096]{0,1:T(8,128)(2,1)} %all-gather.3.cloned.1.call-done), kind=kOutput, calls=%fused_computation.4 | convolution fusion | flops 805404672 | bytes 9371648 | tf_op jit(solution)/shard_map/dot_general | solution.py:8
  244.1 35.0 %all-gather.5.cloned.1.call-done = bf16[768,1024]{1,0:T(8,128)(2,1)} async-done(((bf16[96,1024]{1,0:T(8,128)(2,1)}), bf16[768,1024]{1,0:T(8,128)(2,1)}) %all-gather.5.cloned.1.call-update) | async-done | bytes 1572880 | tf_op jit(solution)/shard_map/all_gather | solution.py:20
  279.1 3.5 collective-permute-start
  282.6 35.3 %collective-permute-done = bf16[768,1024]{1,0:T(8,128)(2,1)S(1)} collective-permute-done((bf16[768,1024]{1,0:T(8,128)(2,1)}, bf16[768,1024]{1,0:T(8,128)(2,1)S(1)}, u32[]{:S(2)}, u32[]{:S(2)}) %collective-permute-start) | collective-permute-done | bytes 1572896 | tf_op jit(solution)/shard_map/ppermute | solution.py:25
  317.8 1.2 copy-done.2
  319.0 3.4 collective-permute-start.1
  322.4 34.5 %collective-permute-done.1 = bf16[768,1024]{1,0:T(8,128)(2,1)} collective-permute-done((bf16[768,1024]{1,0:T(8,128)(2,1)S(1)}, bf16[768,1024]{1,0:T(8,128)(2,1)}, u32[]{:S(2)}, u32[]{:S(2)}) %collective-permute-start.1) | collective-permute-done | bytes 1572896 | tf_op jit(solution)/shard_map/ppermute | solution.py:25
  356.8 3.3 collective-permute-start.2
  360.9 34.6 %collective-permute-done.2 = bf16[768,1024]{1,0:T(8,128)(2,1)} collective-permute-done((bf16[768,1024]{1,0:T(8,128)(2,1)}, bf16[768,1024]{1,0:T(8,128)(2,1)}, u32[]{:S(2)}, u32[]{:S(2)}) %collective-permute-start.2) | collective-permute-done | bytes 1572896 | tf_op jit(solution)/shard_map/ppermute | solution.py:25
  395.4 1.5 constant_dynamic-update-slice_fusion.7
  397.0 1.6 constant_dynamic-update-slice_fusion.6
  398.6 1.5 constant_dynamic-update-slice_fusion.5
  400.2 0.1 constant_dynamic-update-slice_fusion.4
  400.3 1.5 constant_dynamic-update-slice_fusion.3
  401.8 1.5 constant_dynamic-update-slice_fusion.2
  403.4 0.1 constant_dynamic-update-slice_fusion.1
  403.5 0.1 constant_dynamic-update-slice_fusion
  403.6 3.1 constant_dynamic-slice_fusion
  406.7 8.6 %copy.6 = bf16[768,4096]{0,1:T(8,128)(2,1)} copy(bf16[768,4096]{1,0:T(8,128)(2,1)} %constant_dynamic-slice_fusion) | data formatting | bytes 12582912 | tf_op jit(solution)/shard_map/jit(_roll_dynamic)/dynamic_slice | solution.py:26
  415.4 6.0 %gather_fusion = bf16[512,768]{1,0:T(8,128)(2,1)S(1)} fusion(bf16[768,4096]{0,1:T(8,128)(2,1)} %copy.6, s32[1024]{0:T(1024)S(1)} %pad_clamp_fusion), kind=kCustom, calls=%fused_computation | custom fusion | bytes 1574912 | tf_op jit(solution)/shard_map/jit(_take)/gather | solution.py:32
  421.4 2.7 fusion
  424.1 74.5 %reduce-scatter.2.cloned.1.call-done = f32[64,512]{1,0:T(8,128)} async-done(((f32[1024,512]{1,0:T(8,128)}), f32[64,512]{1,0:T(8,128)}) %reduce-scatter.2.cloned.1.call-update) | async-done | bytes 131088 | tf_op jit(solution)/shard_map/reduce_scatter | solution.py:36
  (18 shorter events, 0.2 us)
Async XLA Ops:
  6.5 231.9 %copy-start = (bf16[96,4096]{1,0:T(8,128)(2,1)S(1)}, bf16[96,4096]{1,0:T(8,128)(2,1)}, u32[]{:S(2)}) copy-start(bf16[96,4096]{1,0:T(8,128)(2,1)} %param.4) | copy-start | bytes 2359300
  6.5 231.9 %all-gather.3.cloned.1.call-start = ((), (), s32[]{:S(2)}) async-start(), calls=%async_computation.1 | async-start | bytes 8454144 | tf_op jit(solution)/shard_map/all_gather | solution.py:18
  7.3 353.6 %copy-start.4 = (f32[768]{0:T(1024)S(1)}, f32[768]{0:T(1024)}, u32[]{:S(2)}) copy-start(f32[768]{0:T(1024)} %param.6) | copy-start | bytes 9220
  7.3 271.8 %all-gather.5.cloned.1.call-start = ((), (), s32[]{:S(2)}) async-start(), calls=%async_computation.2 | async-start | bytes 1769472 | tf_op jit(solution)/shard_map/all_gather | solution.py:20
  244.0 254.6 %reduce-scatter.2.cloned.1.call-start = ((), (), s32[]{:S(2)}) async-start(), calls=%async_computation.3 | async-start | bytes 2228224 | tf_op jit(solution)/shard_map/reduce_scatter | solution.py:36
  279.1 121.1 %copy-start.1 = (bf16[768,1024]{1,0:T(8,128)(2,1)S(1)}, bf16[768,1024]{1,0:T(8,128)(2,1)}, u32[]{:S(2)}) copy-start(bf16[768,1024]{1,0:T(8,128)(2,1)} %all-gather.5.cloned.1.call-done) | copy-start | bytes 4718596
  279.1 38.8 %collective-permute-start = (bf16[768,1024]{1,0:T(8,128)(2,1)}, bf16[768,1024]{1,0:T(8,128)(2,1)S(1)}, u32[]{:S(2)}, u32[]{:S(2)}) collective-permute-start(bf16[768,1024]{1,0:T(8,128)(2,1)} %all-gather.5.cloned.1.call-done), channel_id=1, source_target_pairs={{0,8},{8,16},{16,24},{24,0},{1,9},{9,17},{17,25},{25,1},{2,10},{10... | collective-permute-start | bytes 4718600 | tf_op jit(solution)/shard_map/ppermute | solution.py:25
  317.8 1.2 copy-start.2
  319.0 37.8 %collective-permute-start.1 = (bf16[768,1024]{1,0:T(8,128)(2,1)S(1)}, bf16[768,1024]{1,0:T(8,128)(2,1)}, u32[]{:S(2)}, u32[]{:S(2)}) collective-permute-start(bf16[768,1024]{1,0:T(8,128)(2,1)S(1)} %collective-permute-done), channel_id=1, source_target_pairs={{0,8},{8,16},{16,24},{24,0},{1,9},{9,17},{17,25},{25,1},{2,10},{10... | collective-permute-start | bytes 4718600 | tf_op jit(solution)/shard_map/ppermute | solution.py:25
  356.8 38.6 %collective-permute-start.2 = (bf16[768,1024]{1,0:T(8,128)(2,1)}, bf16[768,1024]{1,0:T(8,128)(2,1)}, u32[]{:S(2)}, u32[]{:S(2)}) collective-permute-start(bf16[768,1024]{1,0:T(8,128)(2,1)} %collective-permute-done.1), channel_id=1, source_target_pairs={{0,8},{8,16},{16,24},{24,0},{1,9},{9,17},{17,25},{25,1},{2,10},{10... | collective-permute-start | bytes 4718600 | tf_op jit(solution)/shard_map/ppermute | solution.py:25
  397.0 6.4 %copy-start.3 = (bf16[768,1024]{1,0:T(8,128)(2,1)S(1)}, bf16[768,1024]{1,0:T(8,128)(2,1)}, u32[]{:S(2)}) copy-start(bf16[768,1024]{1,0:T(8,128)(2,1)} %copy-done.2) | copy-start | bytes 4718596
Sparse Core Ops, SparseCore 0:
  9.5 228.9 all-gather.2
  244.1 34.8 all-gather.4
  424.2 74.3 reduce-scatter.1
